TPU v7x, 32 devices: a whole 2x2x4 slice. The times are simulated.
32 devices in a mesh: fsdp: 8 (over y, x, core), tensor: 4 (over z).
Axes of the slice: x: 2, y: 2, z: 4, core: 2. Of those that a mesh axis runs over, the one named last changes fastest.
Arguments:
- hidden_t: bfloat16 [28672, 512], P('fsdp', 'tensor'), may hold values from -6 to 6
- down_weight: bfloat16 [28672, 4096], P('fsdp', 'tensor'), may hold values from -0.03125 to 0.03125
- probe: bfloat16 [28672, 4096], P('fsdp', 'tensor'), may hold values from -5 to 5
- grad_moment: bfloat16 [28672, 4096], P('fsdp', 'tensor'), may hold values from -0.0059814453 to 0.0059814453
- curv_moment: bfloat16 [28672, 4096], P('fsdp', 'tensor'), may hold values from 0.0099487305 to 0.099609375
- target: bfloat16 [512, 4096], P('fsdp', 'tensor'), may hold values from -6 to 6
Outputs:
- new_grad_moment: bfloat16 [28672, 4096], P('fsdp', 'tensor')
- new_curv_moment: bfloat16 [28672, 4096], P('fsdp', 'tensor')
- update: bfloat16 [28672, 4096], P('fsdp', 'tensor')
All inputs are finite; a program needn't handle non-finite values.
Results may differ from a plain program's by a relative error of at most 0.0056.
Values may be sent and summed in bfloat16 or wider, within the bound.
A program may use at most 192 MiB of HBM per device.

v0:
```python
import jax
import jax.numpy as jnp
from jax import lax
from jax.sharding import PartitionSpec as P

BETA_ONE = 0.965
BETA_TWO = 0.99
RHO_SCALE = 0.02
EPS_FLOOR = 0.0005


def cotangents(summed, target_rows, col_width, token_count):
    adjoint = ((summed[:, :col_width] - target_rows.astype(jnp.float32)) / token_count).astype(
        jnp.bfloat16
    )
    tangent_adjoint = (summed[:, col_width:] / token_count).astype(jnp.bfloat16)
    return jnp.concatenate([adjoint, tangent_adjoint], axis=1)


def shards(hidden_t, down_weight, probe, grad_moment, curv_moment, target):
    gathered = lax.all_gather(hidden_t, "tensor", axis=1, tiled=True)
    col_width = down_weight.shape[1]
    token_count = gathered.shape[1]
    paired = jnp.concatenate([down_weight, probe], axis=1)
    partial_out = lax.dot_general(
        gathered, paired, (((0,), (0,)), ((), ())), preferred_element_type=jnp.float32
    )
    totals = lax.psum(partial_out, "fsdp")
    target_all = lax.all_gather(target, "fsdp", axis=0, tiled=True)
    stacked = cotangents(totals, target_all, col_width, token_count)
    products = jnp.dot(gathered, stacked, preferred_element_type=jnp.float32)
    gradient = products[:, :col_width]
    hess_probe = products[:, col_width:]
    estimate = probe.astype(jnp.float32) * hess_probe
    moment_next = BETA_ONE * grad_moment.astype(jnp.float32) + (1.0 - BETA_ONE) * gradient
    curv_next = BETA_TWO * curv_moment.astype(jnp.float32) + (1.0 - BETA_TWO) * estimate
    raw_ratio = moment_next / jnp.maximum(RHO_SCALE * curv_next, EPS_FLOOR)
    update = jnp.clip(raw_ratio, -1.0, 1.0)
    return (
        moment_next.astype(jnp.bfloat16),
        curv_next.astype(jnp.bfloat16),
        update.astype(jnp.bfloat16),
    )


def solution(mesh):
    in_specs = (
        P("fsdp", "tensor"),
        P("fsdp", "tensor"),
        P("fsdp", "tensor"),
        P("fsdp", "tensor"),
        P("fsdp", "tensor"),
        P("fsdp", "tensor"),
    )
    out_specs = (P("fsdp", "tensor"), P("fsdp", "tensor"), P("fsdp", "tensor"))
    return jax.shard_map(shards, mesh=mesh, in_specs=in_specs, out_specs=out_specs, check_vma=False)
```

profile of v0, /device:TPU:0, one launch (start us, length us, event | category | flops | bytes accessed | tf_op | source)
XLA Modules:
  0.0 273.3 jit_solution(6230435863053550682)
XLA Ops:
  7.2 0.0 all-gather.3.cloned.1.call-start
  7.2 0.7 all-gather.3.cloned.1.call-update
  7.9 0.0 all-gather.5.cloned.1.call-start
  7.9 0.7 all-gather.5.cloned.1.call-update
  8.6 0.0 all-reduce.2.cloned.1.call-start
  8.7 75.6 %all-gather.3.cloned.1.call-done = bf16[3584,512]{1,0:T(8,128)(2,1)} async-done(((bf16[3584,128]{1,0:T(8,128)(2,1)}), bf16[3584,512]{1,0:T(8,128)(2,1)}) %all-gather.3.cloned.1.call-update) | async-done | bytes 3670032 | tf_op jit(solution)/shard_map/all_gather | solution.py:21
  84.3 16.0 %fusion.8 = f32[512,2048]{0,1:T(8,128)} fusion(bf16[3584,512]{1,0:T(8,128)(2,1)} %all-gather.3.cloned.1.call-done, bf16[3584,1024]{1,0:T(8,128)(2,1)} %param.8, bf16[3584,1024]{1,0:T(8,128)(2,1)} %param.7), kind=kOutput, calls=%fused_computation.12 | convolution fusion | flops 7545552896 | bytes 22544384 | tf_op jit(solution)/shard_map/dot_general | solution.py:25
  100.3 0.0 all-reduce.2.cloned.1.call-update
  100.3 10.2 %copy.19 = bf16[3584,1024]{0,1:T(8,128)(2,1)} copy(bf16[3584,1024]{1,0:T(8,128)(2,1)} %param.8) | data formatting | bytes 14680064 | tf_op args[2]
  110.6 10.2 %copy.16 = bf16[3584,1024]{0,1:T(8,128)(2,1)} copy(bf16[3584,1024]{1,0:T(8,128)(2,1)} %param.9) | data formatting | bytes 14680064 | tf_op args[3]
  120.7 10.0 %copy.18 = bf16[3584,1024]{0,1:T(8,128)(2,1)} copy(bf16[3584,1024]{1,0:T(8,128)(2,1)} %param.10) | data formatting | bytes 14680064 | tf_op args[4]
  130.8 0.0 all-gather.5.cloned.1.call-done
  130.8 1.5 copy.17
  132.3 59.9 %all-reduce.2.cloned.1.call-done = f32[512,2048]{0,1:T(8,128)} async-done(((f32[512,2048]{0,1:T(8,128)}), f32[512,2048]{0,1:T(8,128)}) %all-reduce.2.cloned.1.call-update) | async-done | bytes 4194320 | tf_op jit(solution)/shard_map/psum | solution.py:28
  192.2 0.0 slice-start
  192.2 3.0 %fusion.14 = (bf16[512,1024]{0,1:T(8,128)(2,1)S(1)}, bf16[512,1024]{0,1:T(8,128)(2,1)S(1)}) fusion(f32[512,2048]{0,1:T(8,128)} %all-reduce.2.cloned.1.call-done, bf16[512,1024]{0,1:T(8,128)(2,1)S(1)} %copy.17), kind=kLoop, calls=%fused_computation.18 | loop fusion | flops 3145728 | bytes 7340032 | tf_op jit(solution)/shard_map/convert_element_type | solution.py:13
  195.2 0.0 slice-start.1
  195.3 16.8 %convolution_bitcast_fusion = f32[3584,2048]{0,1:T(8,128)} fusion(bf16[3584,512]{1,0:T(8,128)(2,1)} %all-gather.3.cloned.1.call-done, bf16[512,1024]{0,1:T(8,128)(2,1)S(1)} %get-tuple-element.13, bf16[512,1024]{0,1:T(8,128)(2,1)S(1)} %get-tuple-element.12), kind=kOutput, calls=%fused_computation | convolution fusion | flops 7520387072 | bytes 35127296 | tf_op jit(solution)/shard_map/dot_general | solution.py:31
  212.1 0.0 slice-done
  212.1 0.0 slice-done.1
  212.1 23.6 %clamp_convert_fusion = (bf16[3584,1024]{0,1:T(8,128)(2,1)}, bf16[3584,1024]{0,1:T(8,128)(2,1)}, bf16[3584,1024]{0,1:T(8,128)(2,1)}) fusion(f32[3584,2048]{0,1:T(8,128)} %convolution_bitcast_fusion, bf16[3584,1024]{0,1:T(8,128)(2,1)} %copy.16, bf16[3584,1024]{0,1:T(8,128)(2,1)S(1)} %bitcast.7, bf16[3584,1024]{0,1:T(8,128)(2,1)} %copy.18), kind=kLoop, calls=%fused_computation.10 | loop fusion | flops 62390272 | bytes 73400320 | tf_op jit(solution)/shard_map/convert_element_type | solution.py:42
  235.6 10.4 %copy.20 = bf16[3584,1024]{1,0:T(8,128)(2,1)} copy(bf16[3584,1024]{0,1:T(8,128)(2,1)} %get-tuple-element.11) | data formatting | bytes 14680064
  246.0 10.4 %copy.21 = bf16[3584,1024]{1,0:T(8,128)(2,1)} copy(bf16[3584,1024]{0,1:T(8,128)(2,1)} %get-tuple-element.10) | data formatting | bytes 14680064
  256.4 10.4 %copy.22 = bf16[3584,1024]{1,0:T(8,128)(2,1)} copy(bf16[3584,1024]{0,1:T(8,128)(2,1)} %get-tuple-element.9) | data formatting | bytes 14680064
  (1 shorter events, 0.0 us)
Async XLA Ops:
  7.2 77.1 %all-gather.3.cloned.1.call-start = ((), (), s32[]{:S(2)}) async-start(), calls=%async_computation | async-start | bytes 4587520 | tf_op jit(solution)/shard_map/all_gather | solution.py:21
  7.9 122.9 %all-gather.5.cloned.1.call-start = ((), (), s32[]{:S(2)}) async-start(), calls=%async_computation.2 | async-start | bytes 1179648 | tf_op jit(solution)/shard_map/all_gather | solution.py:29
  8.6 183.6 %all-reduce.2.cloned.1.call-start = ((), (), s32[]{:S(2)}) async-start(), calls=%async_computation.1 | async-start | bytes 8388608 | tf_op jit(solution)/shard_map/psum | solution.py:28
  192.2 19.9 %slice-start = ((s8[7340032]{0:T(1024)(128)(4,1)}), s8[4194304]{0:T(1024)(128)(4,1)S(1)}, s32[]{:S(2)}) async-start(s8[7340032]{0:T(1024)(128)(4,1)} %bitcast.6), calls=%async_computation.3 | async-start | bytes 8388608
  195.2 16.8 %slice-start.1 = ((s8[7340032]{0:T(1024)(128)(4,1)}), s8[3145728]{0:T(1024)(128)(4,1)S(1)}, s32[]{:S(2)}) async-start(s8[7340032]{0:T(1024)(128)(4,1)} %bitcast.6), calls=%async_computation.4 | async-start | bytes 6291456
Sparse Core Ops, SparseCore 0:
  9.6 74.6 all-gather.2
  86.2 21.6 all-gather.4
  111.2 80.9 all-reduce.1
where the time goes:
time: 275 us; the launch traced here: 273 us
  waiting for transfers between devices  137 us (50%)
  local copies, waits for them, and re-layouts  63.2 us (23%)
  matrix products  32.8 us (12%)
  other arithmetic  26.6 us (10%)
  between operations  13.8 us (5%)
    all_gather x1, waiting for transfers between devices, shards(): gathered = lax.all_gather(hidden_t, 'tensor', axis=1, tiled=True)  75.6 us
    unnamed x10, local copies, waits for them, and re-layouts  61.7 us
    psum x1, waiting for transfers between devices, shards(): totals = lax.psum(partial_out, 'fsdp')  59.9 us
    convert_element_type x1, other arithmetic, shards(): update.astype(jnp.bfloat16)  23.6 us
    dot_general x1, matrix products, shards(): products = jnp.dot(gathered, stacked, preferred_element_type=jnp.float32)  16.8 us
    dot_general x1, matrix products, shards(): lax.dot_general(gathered, paired, (((0,), (0,)), ((), ())), preferred_ele...  16 us
  transfers between devices with their start and end apart: 3, of which 2 were waited for; matrix products, arithmetic and copies ran while one was open for 18% of the time, Pallas kernels for 0%

commit v1 on v0

--- a/solution.py
+++ b/solution.py
@@ -25,7 +25,10 @@
     partial_out = lax.dot_general(
         gathered, paired, (((0,), (0,)), ((), ())), preferred_element_type=jnp.float32
     )
-    totals = lax.psum(partial_out, "fsdp")
+    count, totals = (lax.axis_size("fsdp"), partial_out)
+    for far in [1 << k for k in range(count.bit_length() - 1)]:
+        swap = [(i, i ^ far) for i in range(count)]
+        totals = totals + lax.ppermute(totals, "fsdp", swap)
     target_all = lax.all_gather(target, "fsdp", axis=0, tiled=True)
     stacked = cotangents(totals, target_all, col_width, token_count)
     products = jnp.dot(gathered, stacked, preferred_element_type=jnp.float32)

time: 275 us -> 384 us (1.40)
  waiting for transfers between devices: 137 us -> 239 us
  other arithmetic: 26.6 us -> 32.7 us
    ppermute x0 -> x3, waiting for transfers between devices: none -> 162 us  [shards(): totals = totals + lax.ppermute(totals, 'fsdp', swap)]
    psum x1 -> x0, waiting for transfers between devices: 59.9 us -> none  [shards(): totals = lax.psum(partial_out, 'fsdp')]
    add x0 -> x3, other arithmetic: none -> 8.46 us  [shards(): totals = totals + lax.ppermute(totals, 'fsdp', swap)]
    dot_general x1, matrix products: 16 us -> 12.2 us  [shards(): lax.dot_general(gathered, paired, (((0,), (0,)), ((), ())), preferred_ele...]
  transfers between devices with their start and end apart: 3 -> 5, of which waited for: 2 -> 4; matrix products, arithmetic and copies ran while one was open for 18% -> 8% of each run, Pallas kernels for 0% -> 0%
where the time goes in v1:
time: 384 us; the launch traced here: 382 us
  waiting for transfers between devices  239 us (62%)
  local copies, waits for them, and re-layouts  62.5 us (16%)
  other arithmetic  32.7 us (9%)
  matrix products  29.4 us (8%)
  between operations  15.5 us (4%)
    ppermute x3, waiting for transfers between devices, shards(): totals = totals + lax.ppermute(totals, 'fsdp', swap)  162 us
    all_gather x1, waiting for transfers between devices, shards(): gathered = lax.all_gather(hidden_t, 'tensor', axis=1, tiled=True)  76.3 us
    unnamed x10, local copies, waits for them, and re-layouts  61 us
    convert_element_type x1, other arithmetic, shards(): update.astype(jnp.bfloat16)  23.6 us
    dot_general x1, matrix products, shards(): products = jnp.dot(gathered, stacked, preferred_element_type=jnp.float32)  17.3 us
    dot_general x1, matrix products, shards(): lax.dot_general(gathered, paired, (((0,), (0,)), ((), ())), preferred_ele...  12.2 us
    add x3, other arithmetic, shards(): totals = totals + lax.ppermute(totals, 'fsdp', swap)  8.46 us
  transfers between devices with their start and end apart: 5, of which 4 were waited for; matrix products, arithmetic and copies ran while one was open for 8% of the time, Pallas kernels for 0%

profile of v1, /device:TPU:0, one launch (start us, length us, event | category | flops | bytes accessed | tf_op | source)
XLA Modules:
  0.0 382.2 jit_solution(8380507689736515942)
XLA Ops:
  8.0 0.0 all-gather.3.cloned.1.call-start
  8.0 0.7 all-gather.3.cloned.1.call-update
  8.7 0.0 all-gather.5.cloned.1.call-start
  8.8 76.3 %all-gather.3.cloned.1.call-done = bf16[3584,512]{1,0:T(8,128)(2,1)} async-done(((bf16[3584,128]{1,0:T(8,128)(2,1)}), bf16[3584,512]{1,0:T(8,128)(2,1)}) %all-gather.3.cloned.1.call-update) | async-done | bytes 3670032 | tf_op jit(solution)/shard_map/all_gather | solution.py:21
  85.1 12.2 %fusion.8 = f32[512,2048]{0,1:T(8,128)S(1)} fusion(bf16[3584,512]{1,0:T(8,128)(2,1)} %all-gather.3.cloned.1.call-done, bf16[3584,1024]{1,0:T(8,128)(2,1)} %param.8, bf16[3584,1024]{1,0:T(8,128)(2,1)} %param.7), kind=kOutput, calls=%fused_computation.12 | convolution fusion | flops 7545552896 | bytes 22544384 | tf_op jit(solution)/shard_map/dot_general | solution.py:25
  97.3 0.1 collective-permute-start
  97.4 7.1 %collective-permute-done = f32[512,2048]{0,1:T(8,128)S(1)} collective-permute-done((f32[512,2048]{0,1:T(8,128)S(1)}, f32[512,2048]{0,1:T(8,128)S(1)}, u32[]{:S(2)}, u32[]{:S(2)}) %collective-permute-start) | collective-permute-done | bytes 4194336 | tf_op jit(solution)/shard_map/ppermute | solution.py:31
  104.5 1.0 add.15
  105.5 1.5 collective-permute-start.1
  107.1 91.1 %collective-permute-done.1 = f32[512,2048]{0,1:T(8,128)S(1)} collective-permute-done((f32[512,2048]{0,1:T(8,128)S(1)}, f32[512,2048]{0,1:T(8,128)S(1)}, u32[]{:S(2)}, u32[]{:S(2)}) %collective-permute-start.1) | collective-permute-done | bytes 4194336 | tf_op jit(solution)/shard_map/ppermute | solution.py:31
  198.2 3.0 add.16
  201.2 1.5 collective-permute-start.2
  202.6 0.0 all-gather.5.cloned.1.call-update
  202.7 9.9 %copy.19 = bf16[3584,1024]{0,1:T(8,128)(2,1)} copy(bf16[3584,1024]{1,0:T(8,128)(2,1)} %param.8) | data formatting | bytes 14680064 | tf_op args[2]
  212.6 9.9 %copy.16 = bf16[3584,1024]{0,1:T(8,128)(2,1)} copy(bf16[3584,1024]{1,0:T(8,128)(2,1)} %param.9) | data formatting | bytes 14680064 | tf_op args[3]
  222.5 9.9 %copy.18 = bf16[3584,1024]{0,1:T(8,128)(2,1)} copy(bf16[3584,1024]{1,0:T(8,128)(2,1)} %param.10) | data formatting | bytes 14680064 | tf_op args[4]
  232.5 0.0 all-gather.5.cloned.1.call-done
  232.5 1.5 copy.17
  234.0 63.5 %collective-permute-done.2 = f32[512,2048]{0,1:T(8,128)} collective-permute-done((f32[512,2048]{0,1:T(8,128)}, f32[512,2048]{0,1:T(8,128)}, u32[]{:S(2)}, u32[]{:S(2)}) %collective-permute-start.2) | collective-permute-done | bytes 4194336 | tf_op jit(solution)/shard_map/ppermute | solution.py:31
  297.5 4.5 %add.17 = f32[512,2048]{0,1:T(8,128)S(1)} add(f32[512,2048]{0,1:T(8,128)} %add.16, f32[512,2048]{0,1:T(8,128)} %collective-permute-done.2) | non-fusion elementwise | flops 1048576 | bytes 12582912 | tf_op jit(solution)/shard_map/add | solution.py:31
  302.0 0.0 slice-start
  302.0 0.7 fusion.14
  302.7 0.0 slice-start.1
  302.7 17.3 %convolution_bitcast_fusion = f32[3584,2048]{0,1:T(8,128)} fusion(bf16[3584,512]{1,0:T(8,128)(2,1)} %all-gather.3.cloned.1.call-done, bf16[512,1024]{0,1:T(8,128)(2,1)S(1)} %get-tuple-element.13, bf16[512,1024]{0,1:T(8,128)(2,1)S(1)} %get-tuple-element.12), kind=kOutput, calls=%fused_computation | convolution fusion | flops 7520387072 | bytes 35127296 | tf_op jit(solution)/shard_map/dot_general | solution.py:34
  320.0 0.0 slice-done
  320.0 0.0 slice-done.1
  320.0 23.6 %clamp_convert_fusion = (bf16[3584,1024]{0,1:T(8,128)(2,1)}, bf16[3584,1024]{0,1:T(8,128)(2,1)}, bf16[3584,1024]{0,1:T(8,128)(2,1)}) fusion(f32[3584,2048]{0,1:T(8,128)} %convolution_bitcast_fusion, bf16[3584,1024]{0,1:T(8,128)(2,1)} %copy.16, bf16[3584,1024]{0,1:T(8,128)(2,1)S(1)} %bitcast.7, bf16[3584,1024]{0,1:T(8,128)(2,1)} %copy.18), kind=kLoop, calls=%fused_computation.10 | loop fusion | flops 62390272 | bytes 73400320 | tf_op jit(solution)/shard_map/convert_element_type | solution.py:45
  343.6 10.4 %copy.20 = bf16[3584,1024]{1,0:T(8,128)(2,1)} copy(bf16[3584,1024]{0,1:T(8,128)(2,1)} %get-tuple-element.11) | data formatting | bytes 14680064
  354.0 10.4 %copy.21 = bf16[3584,1024]{1,0:T(8,128)(2,1)} copy(bf16[3584,1024]{0,1:T(8,128)(2,1)} %get-tuple-element.10) | data formatting | bytes 14680064
  364.3 10.4 %copy.22 = bf16[3584,1024]{1,0:T(8,128)(2,1)} copy(bf16[3584,1024]{0,1:T(8,128)(2,1)} %get-tuple-element.9) | data formatting | bytes 14680064
  (1 shorter events, 0.0 us)
Async XLA Ops:
  8.0 77.1 %all-gather.3.cloned.1.call-start = ((), (), s32[]{:S(2)}) async-start(), calls=%async_computation | async-start | bytes 4587520 | tf_op jit(solution)/shard_map/all_gather | solution.py:21
  8.7 223.7 %all-gather.5.cloned.1.call-start = ((), (), s32[]{:S(2)}) async-start(), calls=%async_computation.1 | async-start | bytes 1179648 | tf_op jit(solution)/shard_map/all_gather | solution.py:32
  97.3 7.2 %collective-permute-start = (f32[512,2048]{0,1:T(8,128)S(1)}, f32[512,2048]{0,1:T(8,128)S(1)}, u32[]{:S(2)}, u32[]{:S(2)}) collective-permute-start(f32[512,2048]{0,1:T(8,128)S(1)} %fusion.8), channel_id=1, source_target_pairs={{0,4},{4,0},{8,12},{12,8},{16,20},{20,16},{24,28},{28,24},{1,5},{5... | collective-permute-start | bytes 12582920 | tf_op jit(solution)/shard_map/ppermute | solution.py:31
  105.5 92.7 %collective-permute-start.1 = (f32[512,2048]{0,1:T(8,128)S(1)}, f32[512,2048]{0,1:T(8,128)S(1)}, u32[]{:S(2)}, u32[]{:S(2)}) collective-permute-start(f32[512,2048]{0,1:T(8,128)S(1)} %add.15), channel_id=1, source_target_pairs={{0,8},{4,12},{8,0},{12,4},{16,24},{20,28},{24,16},{28,20},{1,9},{5... | collective-permute-start | bytes 12582920 | tf_op jit(solution)/shard_map/ppermute | solution.py:31
  201.2 96.3 %collective-permute-start.2 = (f32[512,2048]{0,1:T(8,128)}, f32[512,2048]{0,1:T(8,128)}, u32[]{:S(2)}, u32[]{:S(2)}) collective-permute-start(f32[512,2048]{0,1:T(8,128)} %add.16), channel_id=1, source_target_pairs={{0,16},{4,20},{8,24},{12,28},{16,0},{20,4},{24,8},{28,12},{1,17},{... | collective-permute-start | bytes 12582920 | tf_op jit(solution)/shard_map/ppermute | solution.py:31
  302.0 18.0 %slice-start = ((s8[7340032]{0:T(1024)(128)(4,1)}), s8[4194304]{0:T(1024)(128)(4,1)S(1)}, s32[]{:S(2)}) async-start(s8[7340032]{0:T(1024)(128)(4,1)} %bitcast.6), calls=%async_computation.2 | async-start | bytes 8388608
  302.7 17.3 %slice-start.1 = ((s8[7340032]{0:T(1024)(128)(4,1)}), s8[3145728]{0:T(1024)(128)(4,1)S(1)}, s32[]{:S(2)}) async-start(s8[7340032]{0:T(1024)(128)(4,1)} %bitcast.6), calls=%async_computation.3 | async-start | bytes 6291456
Sparse Core Ops, SparseCore 0:
  10.4 74.6 all-gather.2
Sparse Core Ops, SparseCore 1:
  202.7 25.0 all-gather.4
